TPU v7x, 32 devices: a whole 2x2x4 slice. The times are simulated.
32 devices in a mesh: groups: 2 (over y), adapter: 4 (over z), tensor: 4 (over x, core).
Axes of the slice: x: 2, y: 2, z: 4, core: 2. Of those that a mesh axis runs over, the one named last changes fastest.
Arguments:
- tokens: bfloat16 [768, 8192], P(('groups', 'adapter'), 'tensor'), parts along dimension 0, may hold values from -6 to 6
- query_value_weight: bfloat16 [8192, 9216], P('tensor', 'adapter'), may hold values from -0.0625 to 0.0625
- adapter_down_factors: bfloat16 [8, 8192, 128], P('adapter', 'tensor'), may hold values from -0.0625 to 0.0625
- adapter_query_factors: bfloat16 [8, 64, 8192], P('adapter'), may hold values from -0.75 to 0.75
- adapter_value_factors: bfloat16 [8, 64, 1024], P('adapter'), may hold values from -0.75 to 0.75
- adapter_index_rows: int32 [768], P(('groups', 'adapter')), parts along dimension 0, may hold values from 0 to 7, as said below
Outputs:
- qv_out: bfloat16 [768, 9216], P(('groups', 'tensor'), 'adapter'), parts along dimension 0
There are 2 independent parts, one for each index of `groups`. A program takes and returns all parts, laid end to end along the dimension named above; an argument that names none is the same for every part. Nothing has to cross between parts.
Inputs may be any that keep to these rules, and one draw needn't show every extreme that they name: `adapter_index_rows`: the owner of adapter k is k // 2. In every aligned block of 96 rows, at most 48 rows name adapters of one owner, and one owner, the same in every block,, the same in every block, is named by exactly 48 rows in every block.
All inputs are finite; a program needn't handle non-finite values.
Results may differ from a plain program's by a relative error of at most 0.0037.
Values may be sent and summed in bfloat16 or wider, within the bound.
A program may use at most 64 MiB of HBM per device.

v0:
```python
import jax
import jax.numpy as jnp
from jax import lax
from jax.sharding import PartitionSpec as P

KVHEADS = 8


adapter_scale = 0.5


def slot_table(hit, capacity):
    counts = jnp.cumsum(hit.astype(jnp.int32), axis=-1) - 1
    places = jnp.arange(capacity, dtype=jnp.int32)
    match = hit[..., None, :] & (counts[..., None, :] == places[:, None])
    column = jnp.arange(hit.shape[-1], dtype=jnp.int32)
    row_of = jnp.sum(jnp.where(match, column, 0), axis=-1)
    filled = jnp.any(match, axis=-1)
    return (row_of, filled)


def on_device(
    tokens,
    query_value_weight,
    adapter_down_factors,
    adapter_query_factors,
    adapter_value_factors,
    adapter_index_rows,
):
    owners_n = lax.axis_size("adapter")
    tensor_n = lax.axis_size("tensor")
    owner_self = lax.axis_index("adapter")
    tensor_self = lax.axis_index("tensor")
    row_dev = tokens.shape[0]
    local_row_count = adapter_down_factors.shape[0]
    value_rank_slice = adapter_down_factors.shape[2]
    query_rank_slice = value_rank_slice // 2
    capacity = max(2, min(4 * row_dev // owners_n, row_dev // 2))
    group_src = owners_n // tensor_n
    block_cols = query_value_weight.shape[1]
    all_ids = lax.all_gather(adapter_index_rows, "adapter", axis=0, tiled=True).reshape(
        owners_n, row_dev
    )
    owners_all = all_ids // local_row_count
    gathered = lax.all_gather(tokens, "adapter", axis=0, tiled=True)
    base = lax.psum_scatter(
        jnp.dot(gathered, query_value_weight, preferred_element_type=jnp.float32),
        "tensor",
        scatter_dimension=0,
        tiled=True,
    )
    slot_row, slot_ok = slot_table(owners_all == owner_self, capacity)
    slot_ids = jnp.take_along_axis(all_ids, slot_row, axis=1)
    local_pick = (slot_ids - owner_self * local_row_count)[..., None] == jnp.arange(
        local_row_count, dtype=jnp.int32
    )
    select = (local_pick & slot_ok[..., None]).astype(jnp.float32)
    targets = jnp.arange(owners_n, dtype=jnp.int32)[:, None]
    send_row, send_ok = slot_table(
        (adapter_index_rows // local_row_count)[None, :] == targets, capacity
    )
    outgoing = jnp.where(send_ok[..., None], tokens[send_row], jnp.zeros((), tokens.dtype))
    dense = jnp.einsum(
        "scd,kdq->sckq",
        lax.all_to_all(outgoing, "adapter", split_axis=0, concat_axis=0, tiled=True),
        adapter_down_factors,
        preferred_element_type=jnp.float32,
    )
    partial_low = jnp.sum(dense * select[..., None], axis=2)
    accumulated_sum = lax.psum(partial_low, "tensor")
    accumulated_sum = lax.dynamic_slice_in_dim(
        accumulated_sum, tensor_self * group_src, group_src, 0
    )
    reduced_rows = (accumulated_sum * adapter_scale).astype(jnp.bfloat16)
    mine = lax.dynamic_slice_in_dim(select, tensor_self * group_src, group_src, 0).astype(
        jnp.bfloat16
    )
    slots_n = group_src * capacity
    broadcast_rows = (mine[..., None] * reduced_rows[..., None, :]).reshape(
        slots_n, local_row_count, value_rank_slice
    )
    up_query = jnp.einsum(
        "mwn,wnq->mq",
        broadcast_rows[..., :query_rank_slice],
        adapter_query_factors,
        preferred_element_type=jnp.float32,
    )
    up_value = jnp.einsum(
        "mwn,wnq->mq",
        broadcast_rows[..., query_rank_slice:],
        adapter_value_factors,
        preferred_element_type=jnp.float32,
    )
    delta = jnp.concatenate(
        [
            up_query.astype(jnp.bfloat16).reshape(slots_n, KVHEADS, -1),
            up_value.astype(jnp.bfloat16).reshape(slots_n, KVHEADS, -1),
        ],
        axis=2,
    )
    delta = delta.reshape(slots_n, owners_n, block_cols).transpose(1, 0, 2)
    returned = lax.all_to_all(delta, "adapter", split_axis=0, concat_axis=0, tiled=True).reshape(
        owners_n * slots_n, block_cols
    )
    mine_owner = lax.dynamic_slice_in_dim(owners_all, tensor_self * group_src, group_src, 0)
    owner_hit = mine_owner[:, None, :] == jnp.arange(owners_n, dtype=jnp.int32)[None, :, None]
    running = jnp.cumsum(owner_hit.astype(jnp.int32), axis=-1) - 1
    place = jnp.sum(jnp.where(owner_hit, running, 0), axis=1)
    source_off = jnp.arange(group_src, dtype=jnp.int32)[:, None] * capacity
    lookup = (mine_owner * slots_n + source_off + place).reshape(-1)
    delta_rows = jnp.take(returned, lookup, axis=0)
    return (base + delta_rows.astype(jnp.float32)).astype(jnp.bfloat16)


def solution(mesh):
    in_specs = (
        P(("groups", "adapter"), "tensor"),
        P("tensor", "adapter"),
        P("adapter", "tensor", None),
        P("adapter", None, None),
        P("adapter", None, None),
        P(("groups", "adapter")),
    )
    out_specs = P(("groups", "tensor"), "adapter")
    return jax.shard_map(
        on_device, mesh=mesh, in_specs=in_specs, out_specs=out_specs, check_vma=False
    )
```

profile of v0, /device:TPU:0, one launch (start us, length us, event | category | flops | bytes accessed | tf_op | source)
XLA Modules:
  0.0 144.5 jit_solution(10323898229381346286)
XLA Ops:
  7.4 0.7 all-gather.2.cloned.1.call-update
  8.1 0.7 and_select_fusion
  8.8 0.3 reduce_window_sum.30
  9.1 0.1 select_reduce_fusion
  9.3 1.1 gather_fusion
  10.5 0.1 fusion.9
  10.7 1.0 broadcast_select_fusion
  11.7 6.3 %all-to-all-start = ((bf16[4,48,2048]{2,1,0:T(8,128)(2,1)}), bf16[4,48,2048]{2,1,0:T(8,128)(2,1)S(1)}, u32[]{:S(2)}, u32[]{:S(2)}) async-start(bf16[4,48,2048]{2,1,0:T(8,128)(2,1)} %broadcast_select_fusion), calls=%async_computation.1 | async-start | bytes 1572864 | tf_op jit(solution)/shard_map/all_to_all | solution.py:65
  18.0 0.6 dynamic-slice
  19.3 0.2 dynamic-update-slice
  19.5 37.9 %all-reduce = s32[384]{0:T(512)S(1)} all-reduce(s32[384]{0:T(512)S(1)} %dynamic-update-slice), channel_id=1, replica_groups=mesh['groups'=2,'adapter'=4,'tensor'=4] {'adapter'}, use_global_device_ids=true, to_apply=%add | all-reduce | flops 384 | bytes 3072
  57.4 0.1 reshape.295
  57.5 0.3 reduce_window_sum.29
  57.8 0.1 select_reduce_fusion.1
  58.0 2.0 %gather_fusion.2 = s32[192]{0:T(256)S(1)} fusion(s32[4,96]{1,0:T(4,128)S(1)} %reshape.295, s32[192]{0:T(256)S(1)} %reshape.318), kind=kCustom, calls=%fused_computation.2 | custom fusion | bytes 3072 | tf_op jit(solution)/shard_map/jit(take_along_axis)/gather | solution.py:53
  60.1 0.1 fusion.7
  60.3 2.3 %fusion.2 = f32[4,48,128]{2,1,0:T(8,128)} fusion(bf16[2,2048,128]{2,1,0:T(8,128)(2,1)} %param.8, bf16[4,48,2048]{2,1,0:T(8,128)(2,1)S(1)} %all-to-all-done, f32[4,48,2]{1,2,0:T(2,128)S(1)} %and_convert_fusion), kind=kOutput, calls=%fused_computation.8 | convolution fusion | flops 201400320 | bytes 1934848 | tf_op jit(solution)/shard_map/scd,kdq->sckq/dot_general | solution.py:63
  62.6 1.4 all-gather.2.cloned.1.call-done
  64.0 9.8 %fusion.24 = f32[384,2304]{1,0:T(8,128)} fusion(bf16[384,2048]{1,0:T(8,128)(2,1)} %all-gather.2.cloned.1.call-done, bf16[2048,2304]{1,0:T(8,128)(2,1)} %param.7), kind=kOutput, calls=%fused_computation.68 | convolution fusion | flops 3623878656 | bytes 14548992 | tf_op jit(solution)/shard_map/dot_general | solution.py:47
  73.8 18.2 %all-reduce.3.cloned.1.call-done = f32[4,48,128]{2,1,0:T(8,128)} async-done(((f32[4,48,128]{2,1,0:T(8,128)}), f32[4,48,128]{2,1,0:T(8,128)}) %all-reduce.3.cloned.1.call-update) | async-done | bytes 98320 | tf_op jit(solution)/shard_map/psum | solution.py:70
  92.0 0.7 fusion.12
  92.9 0.3 fusion.3
  93.2 0.5 fusion
  93.7 0.4 copy.11
  94.2 1.5 %reshape.299 = bf16[48,4,2304]{2,1,0:T(4,128)(2,1)} reshape(bf16[48,8,1152]{2,1,0:T(8,128)(2,1)S(1)} %pad_maximum_fusion) | data formatting | bytes 1769472 | tf_op jit(solution)/shard_map/reshape | solution.py:101
  95.7 2.2 %copy.14 = bf16[48,4,2304]{2,0,1:T(8,128)(2,1)} copy(bf16[48,4,2304]{2,1,0:T(4,128)(2,1)} %reshape.299) | data formatting | bytes 1769472 | tf_op jit(solution)/shard_map/reshape | solution.py:101
  97.9 4.6 %all-to-all-start.1 = ((bf16[4,48,2304]{2,1,0:T(8,128)(2,1)}), bf16[4,48,2304]{2,1,0:T(8,128)(2,1)S(1)}, u32[]{:S(2)}, u32[]{:S(2)}) async-start(bf16[4,48,2304]{2,1,0:T(8,128)(2,1)} %bitcast.57), calls=%async_computation.2 | async-start | bytes 1769472 | tf_op jit(solution)/shard_map/all_to_all | solution.py:102
  102.5 0.3 reduce_window_sum.28
  102.8 20.8 %all-to-all-done.1 = bf16[4,48,2304]{2,1,0:T(8,128)(2,1)S(1)} async-done(((bf16[4,48,2304]{2,1,0:T(8,128)(2,1)}), bf16[4,48,2304]{2,1,0:T(8,128)(2,1)S(1)}, u32[]{:S(2)}, u32[]{:S(2)}) %all-to-all-start.1) | async-done | bytes 884768 | tf_op jit(solution)/shard_map/all_to_all | solution.py:102
  123.6 0.9 gather_fusion.1
  124.4 10.5 %reduce-scatter.2.cloned.1.call-done = f32[96,2304]{1,0:T(8,128)} async-done(((f32[384,2304]{1,0:T(8,128)}), f32[96,2304]{1,0:T(8,128)}) %reduce-scatter.2.cloned.1.call-update) | async-done | bytes 884752 | tf_op jit(solution)/shard_map/reduce_scatter | solution.py:46
  134.9 2.1 %add_convert_fusion = bf16[96,2304]{1,0:T(8,128)(2,1)} fusion(f32[96,2304]{1,0:T(8,128)} %reduce-scatter.2.cloned.1.call-done, bf16[96,2304]{1,0:T(8,128)(2,1)S(1)} %gather_fusion.1, pred[96]{0:T(512)(128)(4,1)S(1)} %get-tuple-element.5), kind=kLoop, calls=%fused_computation.13 | loop fusion | flops 884736 | bytes 1769568 | tf_op jit(solution)/shard_map/convert_element_type | solution.py:112
  (39 shorter events, 0.7 us)
Async XLA Ops:
  7.4 85.8 %copy-start = (bf16[2,64,8192]{2,1,0:T(8,128)(2,1)S(1)}, bf16[2,64,8192]{2,1,0:T(8,128)(2,1)}, u32[]{:S(2)}) copy-start(bf16[2,64,8192]{2,1,0:T(8,128)(2,1)} %param.9) | copy-start | bytes 6291460
  7.4 2.0 %copy-start.1 = (bf16[96,2048]{1,0:T(8,128)(2,1)S(1)}, bf16[96,2048]{1,0:T(8,128)(2,1)}, u32[]{:S(2)}) copy-start(bf16[96,2048]{1,0:T(8,128)(2,1)} %param.6) | copy-start | bytes 1179652
  7.4 56.6 %all-gather.2.cloned.1.call-start = ((), (), s32[]{:S(2)}) async-start(), calls=%async_computation.3 | async-start | bytes 1966080 | tf_op jit(solution)/shard_map/all_gather | solution.py:45
  10.5 7.5 %copy-start.4 = (u32[32]{0:T(128)S(1)}, u32[32]{0:T(128)}, u32[]{:S(2)}) copy-start(u32[32]{0:T(128)} %constant.106) | copy-start | bytes 388
  10.5 8.7 %copy-start.3 = (s32[96]{0:T(128)S(1)}, s32[96]{0:T(128)}, u32[]{:S(2)}) copy-start(s32[96]{0:T(128)} %param.11) | copy-start | bytes 1156
  11.7 48.6 %all-to-all-start = ((bf16[4,48,2048]{2,1,0:T(8,128)(2,1)}), bf16[4,48,2048]{2,1,0:T(8,128)(2,1)S(1)}, u32[]{:S(2)}, u32[]{:S(2)}) async-start(bf16[4,48,2048]{2,1,0:T(8,128)(2,1)} %broadcast_select_fusion), calls=%async_computation.1 | async-start | bytes 1572864 | tf_op jit(solution)/shard_map/all_to_all | solution.py:65
  18.0 74.0 %all-reduce.3.cloned.1.call-start = ((), (), s32[]{:S(2)}) async-start(), calls=%async_computation.5 | async-start | bytes 196608 | tf_op jit(solution)/shard_map/psum | solution.py:70
  62.6 72.4 %reduce-scatter.2.cloned.1.call-start = ((), (), s32[]{:S(2)}) async-start(), calls=%async_computation.4 | async-start | bytes 4423680 | tf_op jit(solution)/shard_map/reduce_scatter | solution.py:46
  73.8 19.1 %copy-start.2 = (bf16[2,64,1024]{2,1,0:T(8,128)(2,1)S(1)}, bf16[2,64,1024]{2,1,0:T(8,128)(2,1)}, u32[]{:S(2)}) copy-start(bf16[2,64,1024]{2,1,0:T(8,128)(2,1)} %param.10) | copy-start | bytes 786436
  97.9 25.7 %all-to-all-start.1 = ((bf16[4,48,2304]{2,1,0:T(8,128)(2,1)}), bf16[4,48,2304]{2,1,0:T(8,128)(2,1)S(1)}, u32[]{:S(2)}, u32[]{:S(2)}) async-start(bf16[4,48,2304]{2,1,0:T(8,128)(2,1)} %bitcast.57), calls=%async_computation.2 | async-start | bytes 1769472 | tf_op jit(solution)/shard_map/all_to_all | solution.py:102
Sparse Core Ops, SparseCore 0:
  9.8 54.1 all-gather.1
Sparse Core Ops, SparseCore 1:
  62.6 29.3 all-reduce.2
  94.6 40.2 reduce-scatter.1
where the time goes:
time: 145 us; the launch traced here: 144 us
  waiting for transfers between devices  51.6 us (36%)
  blocking collectives  37.9 us (26%)
  between operations  15.7 us (11%)
  matrix products  12.8 us (9%)
  starting transfers between devices  11 us (8%)
  local copies, waits for them, and re-layouts  9.31 us (6%)
  other arithmetic  6.23 us (4%)
    unnamed x1, blocking collectives  37.9 us
    all_to_all x1, waiting for transfers between devices, on_device(): lax.all_to_all(delta, 'adapter', split_axis=0, concat_axis=0, tiled=True)  20.8 us
    psum x1, waiting for transfers between devices, on_device(): accumulated_sum = lax.psum(partial_low, 'tensor')  18.2 us
    reduce_scatter x1, waiting for transfers between devices, on_device(): lax.psum_scatter(jnp.dot(gathered, query_value_weight, preferred_element_...  10.5 us
    dot_general x1, matrix products, on_device(): jnp.dot(gathered, query_value_weight, preferred_element_type=jnp.float32)  9.76 us
    all_to_all x1, starting transfers between devices, on_device(): lax.all_to_all(outgoing, 'adapter', split_axis=0, concat_axis=0, tiled=True)  6.32 us
    all_to_all x1, starting transfers between devices, on_device(): lax.all_to_all(delta, 'adapter', split_axis=0, concat_axis=0, tiled=True)  4.6 us
    reshape x2, local copies, waits for them, and re-layouts, on_device(): delta = delta.reshape(slots_n, owners_n, block_cols).transpose(1, 0, 2)  3.68 us
  transfers between devices with their start and end apart: 5, of which 4 were waited for; matrix products, arithmetic and copies ran while one was open for 18% of the time, Pallas kernels for 0%

commit v1 on v0

--- a/solution.py
+++ b/solution.py
@@ -1,6 +1,8 @@
 import jax
 import jax.numpy as jnp
 from jax import lax
+from jax.experimental import pallas as pl
+from jax.experimental.pallas import tpu as pltpu
 from jax.sharding import PartitionSpec as P
 
 KVHEADS = 8
@@ -112,7 +114,322 @@
     return (base + delta_rows.astype(jnp.float32)).astype(jnp.bfloat16)
 
 
+MESH = pl.DeviceIdType.MESH
+ZN = 4
+
+
+def remote(src, dst, send_sem, recv_sem, device):
+    return pltpu.make_async_remote_copy(
+        src_ref=src,
+        dst_ref=dst,
+        send_sem=send_sem,
+        recv_sem=recv_sem,
+        device_id=device,
+        device_id_type=MESH,
+    )
+
+
+def fused_kernel(
+    tok_ref, w_ref, down_ref, bq_ref, bv_ref, ids_ref, out_ref,
+    x, wd, send, recv, base, low_send, low_recv, low_z, ball, ids,
+    load_sem, own_sem, right_s, left_s, x_r, ids_s, ids_r, part_s, part_r,
+    low_s, low_r, lz_s, lz_r, bqz_s, bqz_r, bvz_s, bvz_r, plane_s, plane_r,
+):
+    g = lax.axis_index("groups")
+    a = lax.axis_index("adapter")
+    t = lax.axis_index("tensor")
+    cols = w_ref.shape[1]
+    qcols = bq_ref.shape[2] // ZN
+    vcols = bv_ref.shape[2] // ZN
+    rank = bq_ref.shape[1]
+    rows = tok_ref.shape[0]
+    groups_here = KVHEADS // ZN
+    qg, vg = qcols // groups_here, vcols // groups_here
+    zdev = [lax.rem(a + d, ZN) for d in range(ZN)]
+    tdev = [lax.rem(t + d, ZN) for d in range(ZN)]
+    xpeer = lax.rem(t + 2, ZN)
+    core = lax.rem(t, 2)
+    sibling = t + 1 - 2 * core
+
+    loads = [
+        pltpu.make_async_copy(w_ref, wd.at[:, pl.ds(0, cols)], load_sem.at[0]),
+        pltpu.make_async_copy(down_ref.at[0], wd.at[:, pl.ds(cols, 2 * rank)], load_sem.at[1]),
+        pltpu.make_async_copy(
+            down_ref.at[1], wd.at[:, pl.ds(cols + 2 * rank, 2 * rank)], load_sem.at[2]
+        ),
+        pltpu.make_async_copy(tok_ref, x.at[a], load_sem.at[3]),
+    ]
+    for copy in loads:
+        copy.start()
+    own_q = pl.ds(pl.multiple_of(a * qcols, 128), qcols)
+    own_v = pl.ds(pl.multiple_of(a * vcols, 128), vcols)
+    owns = []
+    for k in range(2):
+        at = pl.ds(k * rank, rank)
+        owns.append(pltpu.make_async_copy(
+            bq_ref.at[k, :, own_q], ball.at[ZN - 1, at, pl.ds(0, qcols)], own_sem.at[2 * k]))
+        owns.append(pltpu.make_async_copy(
+            bv_ref.at[k, :, own_v], ball.at[ZN - 1, at, pl.ds(qcols, vcols)], own_sem.at[2 * k + 1]))
+    for copy in owns:
+        copy.start()
+    ids[pl.ds(a, 1)] = ids_ref[...][None]
+
+    barrier = pltpu.get_barrier_semaphore()
+    for d in range(1, ZN):
+        pl.semaphore_signal(barrier, inc=1, device_id={"adapter": zdev[d]}, device_id_type=MESH)
+        pl.semaphore_signal(barrier, inc=1, device_id={"tensor": tdev[d]}, device_id_type=MESH)
+    pl.semaphore_signal(barrier, inc=1, device_id={"groups": 1 - g}, device_id_type=MESH)
+    pl.semaphore_wait(barrier, 2 * ZN - 1)
+
+    def to_right(src, b):
+        return remote(src, x.at[b], right_s.at[b], x_r.at[b], {"adapter": lax.rem(a + 1, ZN)})
+
+    def to_left(src, b):
+        return remote(src, x.at[b], left_s.at[b], x_r.at[b], {"adapter": lax.rem(a + ZN - 1, ZN)})
+
+    @pl.when(a < ZN - 1)
+    def _():
+        to_right(tok_ref, a).start()
+
+    @pl.when(a > 0)
+    def _():
+        to_left(tok_ref, a).start()
+
+    part = ball.shape[1] // (2 * ZN)
+    p = 2 * t + g
+    p_rows = pl.ds(pl.multiple_of(p * part, part), part)
+    k_src = t // 2
+    r_src = pl.ds(pl.multiple_of((2 * core + g) * part, part), part)
+
+    def ids_copy(d):
+        return remote(ids_ref, ids.at[a], ids_s.at[d], ids_r.at[a], {"adapter": zdev[d]})
+
+    def bq_copy(d):
+        at = pl.ds(pl.multiple_of(zdev[d] * qcols, 128), qcols)
+        return remote(bq_ref.at[k_src, r_src, at], ball.at[d - 1, p_rows, pl.ds(0, qcols)],
+                      bqz_s.at[d], bqz_r.at[d], {"adapter": zdev[d]})
+
+    def bv_copy(d):
+        at = pl.ds(pl.multiple_of(zdev[d] * vcols, 128), vcols)
+        return remote(bv_ref.at[k_src, r_src, at], ball.at[d - 1, p_rows, pl.ds(qcols, vcols)],
+                      bvz_s.at[d], bvz_r.at[d], {"adapter": zdev[d]})
+
+    for d in range(1, ZN):
+        ids_copy(d).start()
+    for d in range(1, ZN):
+        bq_copy(d).start()
+        bv_copy(d).start()
+
+    def y_copy():
+        ref = ball.at[pl.ds(0, ZN - 1), p_rows, :]
+        return remote(ref, ref, plane_s.at[0], plane_r.at[0], {"groups": 1 - g})
+
+    def t_rows(owner_t):
+        return ball.at[pl.ds(0, ZN - 1), pl.ds(pl.multiple_of(owner_t * 2 * part, 2 * part), 2 * part), :]
+
+    def x_copy(owner_t):
+        ref = t_rows(owner_t)
+        return remote(ref, ref, plane_s.at[1], plane_r.at[1], {"tensor": xpeer})
+
+    def core_copy(i, owner_t):
+        ref = t_rows(owner_t)
+        return remote(ref, ref, plane_s.at[2 + i], plane_r.at[2 + i], {"tensor": sibling})
+
+    def column(b):
+        lane = lax.broadcasted_iota(jnp.int32, (rows, 128), 1)
+        row = lax.broadcasted_iota(jnp.int32, (rows, 128), 0)
+        ids_b = jnp.broadcast_to(ids[b][0:1, :], (rows, 128))
+        return jnp.sum(jnp.where(lane == row, ids_b, 0), axis=1, keepdims=True)
+
+    def part_copy(b):
+        return remote(send.at[b], recv.at[t], part_s.at[b], part_r.at[t], {"tensor": b})
+
+    def low_copy(b):
+        return remote(low_send.at[b], low_recv.at[t], low_s.at[b], low_r.at[t], {"tensor": b})
+
+    tile = 256
+
+    def compute(b):
+        both = jnp.dot(x[b], wd[:, cols:], preferred_element_type=jnp.float32)
+        id_col = column(b)
+        zero = jnp.zeros((rows, 2 * rank), jnp.float32)
+        low = jnp.where(id_col == 2 * a, both[:, : 2 * rank], zero)
+        low = jnp.where(id_col == 2 * a + 1, both[:, 2 * rank :], low)
+        low_send[b] = low
+
+        @pl.when(b != t)
+        def _():
+            low_copy(b).start()
+
+            @pl.loop(0, cols // tile)
+            def _(n):
+                at = pl.ds(pl.multiple_of(n * tile, tile), tile)
+                send[b, :, at] = jnp.dot(
+                    x[b], wd[:, at], preferred_element_type=jnp.float32
+                ).astype(jnp.bfloat16)
+
+            part_copy(b).start()
+
+        @pl.when(b == t)
+        def _():
+            @pl.loop(0, cols // tile)
+            def _(n):
+                at = pl.ds(pl.multiple_of(n * tile, tile), tile)
+                base[:, at] = jnp.dot(x[b], wd[:, at], preferred_element_type=jnp.float32)
+
+    for copy in loads:
+        copy.wait()
+    compute(a)
+
+    for d in range(1, ZN):
+        bq_copy(d).wait_recv()
+        bv_copy(d).wait_recv()
+    y_copy().start()
+
+    for s in range(1, ZN):
+        lo, hi = a - s, a + s
+
+        @pl.when(lo >= 0)
+        def _():
+            to_right(tok_ref, lo).wait_recv()
+
+            @pl.when(a < ZN - 1)
+            def _():
+                to_right(x.at[lo], lo).start()
+
+        @pl.when(hi < ZN)
+        def _():
+            to_left(tok_ref, hi).wait_recv()
+
+            @pl.when(a > 0)
+            def _():
+                to_left(x.at[hi], hi).start()
+
+        @pl.loop(0, 2)
+        def _(way):
+            b = a - s + 2 * s * way
+
+            @pl.when((b >= 0) & (b < ZN))
+            def _():
+                remote(ids_ref, ids.at[b], ids_s.at[1], ids_r.at[b], {"adapter": zdev[1]}).wait_recv()
+                compute(b)
+
+        if s == 1:
+            y_copy_in = ball.at[pl.ds(0, ZN - 1), pl.ds(pl.multiple_of((2 * t + 1 - g) * part, part), part), :]
+            remote(y_copy_in, y_copy_in, plane_s.at[0], plane_r.at[0], {"groups": 1 - g}).wait_recv()
+            x_copy(t).start()
+        if s == 2:
+            x_copy(xpeer).wait_recv()
+            core_copy(0, t).start()
+            core_copy(1, xpeer).start()
+
+    total = low_send[t]
+    for d in range(1, ZN):
+        remote(low_send.at[0], low_recv.at[tdev[d]], low_s.at[0], low_r.at[tdev[d]], {"tensor": tdev[d]}).wait_recv()
+        total = total + low_recv[tdev[d]]
+    low_z[0] = (total * adapter_scale).astype(jnp.bfloat16)
+
+    def lz_copy(d):
+        return remote(low_z.at[0], low_z.at[d], lz_s.at[d], lz_r.at[d], {"adapter": zdev[d]})
+
+    for d in range(1, ZN):
+        lz_copy(d).start()
+    for copy in owns:
+        copy.wait()
+    core_copy(0, sibling).wait_recv()
+    core_copy(1, lax.rem(sibling + 2, ZN)).wait_recv()
+    id_col = column(t)
+    low = low_z[0].astype(jnp.float32)
+    for d in range(1, ZN):
+        lz_copy(d).wait_recv()
+        low = low + low_z[d].astype(jnp.float32)
+    wide = jnp.concatenate([low[:, :rank], low[:, :rank]], axis=1)
+    wide_v = jnp.concatenate([low[:, rank:], low[:, rank:]], axis=1)
+    second = lax.broadcasted_iota(jnp.int32, (rows, 2 * rank), 1) // rank
+    lq, lv = [], []
+    for slot in range(ZN):
+        owner = zdev[(ZN - 1 - slot) % ZN]
+        hit = id_col == 2 * owner + second
+        lq.append(jnp.where(hit, wide, 0.0).astype(jnp.bfloat16))
+        lv.append(jnp.where(hit, wide_v, 0.0).astype(jnp.bfloat16))
+    lq = jnp.concatenate(lq, axis=1)
+    lv = jnp.concatenate(lv, axis=1)
+    for d in range(1, ZN):
+        remote(send.at[0], recv.at[tdev[d]], part_s.at[0], part_r.at[tdev[d]], {"tensor": tdev[d]}).wait_recv()
+
+    def finish(at, low_rows, b_at, width):
+        factors = ball[:, :, b_at : b_at + width].reshape(ZN * 2 * rank, width)
+        delta = jnp.dot(low_rows, factors, preferred_element_type=jnp.float32)
+        val = base[:, at : at + width]
+        for d in range(1, ZN):
+            val = val + recv[tdev[d], :, at : at + width].astype(jnp.float32)
+        delta = delta.astype(jnp.bfloat16).astype(jnp.float32)
+        out_ref[:, at : at + width] = (val + delta).astype(jnp.bfloat16)
+
+    for grp in range(groups_here):
+        for c in range(qg // 256):
+            finish(grp * (qg + vg) + c * 256, lq, grp * qg + c * 256, 256)
+        finish(grp * (qg + vg) + qg, lv, qcols + grp * vg, vg)
+
+    @pl.loop(0, ZN)
+    def _(b):
+        @pl.when((b <= a) & (a < ZN - 1))
+        def _():
+            to_right(tok_ref, b).wait_send()
+
+        @pl.when((b >= a) & (a > 0))
+        def _():
+            to_left(tok_ref, b).wait_send()
+
+        @pl.when(b != t)
+        def _():
+            part_copy(b).wait_send()
+            low_copy(b).wait_send()
+
+    for d in range(1, ZN):
+        ids_copy(d).wait_send()
+        bq_copy(d).wait_send()
+        bv_copy(d).wait_send()
+        lz_copy(d).wait_send()
+    y_copy().wait_send()
+    x_copy(t).wait_send()
+    core_copy(0, t).wait_send()
+    core_copy(1, xpeer).wait_send()
+
+
+def fused_on_device(tokens, weight, down, bq, bv, index_rows):
+    rows, feats = tokens.shape
+    cols = weight.shape[1]
+    rank2 = down.shape[2]
+    ids = jnp.broadcast_to(jnp.pad(index_rows, (0, 128 - rows))[None, :], (8, 128))
+    dma = pltpu.SemaphoreType.DMA
+    vmem = pltpu.VMEM
+    any_spec = pl.BlockSpec(memory_space=pl.ANY)
+    return pl.pallas_call(
+        fused_kernel,
+        out_shape=jax.ShapeDtypeStruct((rows, cols), jnp.bfloat16),
+        in_specs=[any_spec] * 5 + [pl.BlockSpec(memory_space=pltpu.VMEM)],
+        out_specs=pl.BlockSpec(memory_space=pltpu.VMEM),
+        scratch_shapes=[
+            vmem((ZN, rows, feats), jnp.bfloat16),
+            vmem((feats, cols + 2 * rank2), jnp.bfloat16),
+            vmem((ZN, rows, cols), jnp.bfloat16),
+            vmem((ZN, rows, cols), jnp.bfloat16),
+            vmem((rows, cols), jnp.float32),
+            vmem((ZN, rows, rank2), jnp.float32),
+            vmem((ZN, rows, rank2), jnp.float32),
+            vmem((ZN, rows, rank2), jnp.bfloat16),
+            vmem((ZN, rank2, cols), jnp.bfloat16),
+            vmem((ZN, 8, 128), jnp.int32),
+        ] + [dma((4,))] * 19,
+        compiler_params=pltpu.CompilerParams(
+            collective_id=0, has_side_effects=True, vmem_limit_bytes=48 * 1024 * 1024
+        ),
+    )(tokens, weight, down, bq, bv, ids)
+
+
 def solution(mesh):
+    fused = (mesh.shape["groups"], mesh.shape["adapter"], mesh.shape["tensor"]) == (2, ZN, ZN)
     in_specs = (
         P(("groups", "adapter"), "tensor"),
         P("tensor", "adapter"),
@@ -123,5 +440,6 @@
     )
     out_specs = P(("groups", "tensor"), "adapter")
     return jax.shard_map(
-        on_device, mesh=mesh, in_specs=in_specs, out_specs=out_specs, check_vma=False
-    )
+        fused_on_device if fused else on_device,
+        mesh=mesh, in_specs=in_specs, out_specs=out_specs, check_vma=False,
+    )

time: 145 us -> 64.1 us (0.44)
  the two profiles are of different devices: /device:TPU:0 before, /device:TPU:11 now
where the time goes in v1:
time: 64.1 us; the launch traced here: 63.8 us
  Pallas kernels  57.6 us (90%)
  local copies, waits for them, and re-layouts  6.19 us (10%)
    pallas_call x1, Pallas kernels, fused_on_device(): pl.pallas_call(fused_kernel, out_shape=jax.ShapeDtypeStruct((rows, cols),...  57.6 us
    unnamed x9, local copies, waits for them, and re-layouts  5.52 us

profile of v1, /device:TPU:11, one launch (start us, length us, event | category | flops | bytes accessed | tf_op | source)
XLA Modules:
  0.0 63.8 jit_solution(8547885563913530693)
XLA Ops:
  0.0 0.7 %pad.4 = s32[128]{0:T(128)S(1)} pad(s32[96]{0:T(128)} %param.11, s32[]{:T(128)} %constant.0.clone.1), padding=0_32 | pad | bytes 900 | tf_op jit(solution)/shard_map/jit(_pad)/pad | solution.py:404
  0.7 0.0 copy-start
  0.7 1.6 %copy-done = bf16[2,64,8192]{2,1,0:T(8,128)(2,1)S(1)} copy-done((bf16[2,64,8192]{2,1,0:T(8,128)(2,1)S(1)}, bf16[2,64,8192]{2,1,0:T(8,128)(2,1)}, u32[]{:S(2)}) %copy-start) | copy-done | bytes 2097176
  2.3 0.0 copy-start.1
  2.3 1.2 %copy-done.1 = bf16[2,2048,128]{2,1,0:T(8,128)(2,1)S(1)} copy-done((bf16[2,2048,128]{2,1,0:T(8,128)(2,1)S(1)}, bf16[2,2048,128]{2,1,0:T(8,128)(2,1)}, u32[]{:S(2)}) %copy-start.1) | copy-done | bytes 1048600
  3.5 0.0 copy-start.2
  3.5 1.0 %copy-done.2 = bf16[96,2048]{1,0:T(8,128)(2,1)S(1)} copy-done((bf16[96,2048]{1,0:T(8,128)(2,1)S(1)}, bf16[96,2048]{1,0:T(8,128)(2,1)}, u32[]{:S(2)}) %copy-start.2) | copy-done | bytes 393240
  4.5 0.0 copy-start.3
  4.5 0.9 %copy-done.3 = bf16[2,64,1024]{2,1,0:T(8,128)(2,1)S(1)} copy-done((bf16[2,64,1024]{2,1,0:T(8,128)(2,1)S(1)}, bf16[2,64,1024]{2,1,0:T(8,128)(2,1)}, u32[]{:S(2)}) %copy-start.3) | copy-done | bytes 262168
  5.4 57.6 %shard_map.64 = bf16[96,2304]{1,0:T(8,128)(2,1)S(1)} custom-call(bf16[96,2048]{1,0:T(8,128)(2,1)S(1)} %copy-done.2, bf16[2048,2304]{1,0:T(8,128)(2,1)} %w_ref.1, bf16[2,2048,128]{2,1,0:T(8,128)(2,1)S(1)} %copy-done.1, bf16[2,64,8192]{2,1,0:T(8,128)(2,1)S(1)} %copy-done, bf16[2,64,1024]{2,1,0:T(8,128)(2,1)S(1)} %copy-done.3, s32[8,128]{1,0:T(8,128)S(1)} %broadcast_in_dim.2.ids_ref), custom_call_target="tpu_custom_call" | custom-call | tf_op jit(solution)/shard_map/pallas_call | solution.py:408
  63.1 0.8 %copy.8 = bf16[96,2304]{1,0:T(8,128)(2,1)} copy(bf16[96,2304]{1,0:T(8,128)(2,1)S(1)} %shard_map.64) | data formatting | bytes 884736
  (1 shorter events, 0.0 us)
Async XLA Ops:
  0.7 1.6 %copy-start = (bf16[2,64,8192]{2,1,0:T(8,128)(2,1)S(1)}, bf16[2,64,8192]{2,1,0:T(8,128)(2,1)}, u32[]{:S(2)}) copy-start(bf16[2,64,8192]{2,1,0:T(8,128)(2,1)} %bq_ref.1) | copy-start | bytes 6291460
  2.3 1.2 %copy-start.1 = (bf16[2,2048,128]{2,1,0:T(8,128)(2,1)S(1)}, bf16[2,2048,128]{2,1,0:T(8,128)(2,1)}, u32[]{:S(2)}) copy-start(bf16[2,2048,128]{2,1,0:T(8,128)(2,1)} %down_ref.1) | copy-start | bytes 3145732
  3.5 1.0 %copy-start.2 = (bf16[96,2048]{1,0:T(8,128)(2,1)S(1)}, bf16[96,2048]{1,0:T(8,128)(2,1)}, u32[]{:S(2)}) copy-start(bf16[96,2048]{1,0:T(8,128)(2,1)} %tok_ref.1) | copy-start | bytes 1179652
  4.5 0.9 %copy-start.3 = (bf16[2,64,1024]{2,1,0:T(8,128)(2,1)S(1)}, bf16[2,64,1024]{2,1,0:T(8,128)(2,1)}, u32[]{:S(2)}) copy-start(bf16[2,64,1024]{2,1,0:T(8,128)(2,1)} %bv_ref.1) | copy-start | bytes 786436

commit v2 on v1

--- a/solution.py
+++ b/solution.py
@@ -115,6 +115,7 @@
 
 
 MESH = pl.DeviceIdType.MESH
+CHUNKS = 3
 ZN = 4
 
 
@@ -131,9 +132,9 @@
 
 def fused_kernel(
     tok_ref, w_ref, down_ref, bq_ref, bv_ref, ids_ref, out_ref,
-    x, wd, send, recv, base, low_send, low_recv, low_z, ball, ids,
-    load_sem, own_sem, right_s, left_s, x_r, ids_s, ids_r, part_s, part_r,
-    low_s, low_r, lz_s, lz_r, bqz_s, bqz_r, bvz_s, bvz_r, plane_s, plane_r,
+    x, wd, pair_send, pair_recv, far_send, far_recv, near_send, near_recv, held, base, low_send, low_recv, low_z, ball, ids,
+    load_sem, own_sem, ids_s, ids_r, pair_s, pair_r, far_s, far_r, near_s, near_r,
+    low_s, low_r, lz_s, lz_r, bqz_s, bqz_r, bvz_s, bvz_r, plane_s, plane_r, right_s, left_s, x_r,
 ):
     g = lax.axis_index("groups")
     a = lax.axis_index("adapter")
@@ -172,7 +173,8 @@
             bv_ref.at[k, :, own_v], ball.at[ZN - 1, at, pl.ds(qcols, vcols)], own_sem.at[2 * k + 1]))
     for copy in owns:
         copy.start()
-    ids[pl.ds(a, 1)] = ids_ref[...][None]
+    ids[a] = jnp.zeros((8, 128), jnp.int32)
+    ids[a, 0:1, 0:rows] = ids_ref[...]
 
     barrier = pltpu.get_barrier_semaphore()
     for d in range(1, ZN):
@@ -181,19 +183,26 @@
     pl.semaphore_signal(barrier, inc=1, device_id={"groups": 1 - g}, device_id_type=MESH)
     pl.semaphore_wait(barrier, 2 * ZN - 1)
 
-    def to_right(src, b):
-        return remote(src, x.at[b], right_s.at[b], x_r.at[b], {"adapter": lax.rem(a + 1, ZN)})
-
-    def to_left(src, b):
-        return remote(src, x.at[b], left_s.at[b], x_r.at[b], {"adapter": lax.rem(a + ZN - 1, ZN)})
-
-    @pl.when(a < ZN - 1)
-    def _():
-        to_right(tok_ref, a).start()
-
-    @pl.when(a > 0)
-    def _():
-        to_left(tok_ref, a).start()
+    step = rows // CHUNKS
+
+    def to_right(src, b, i):
+        at = pl.ds(i * step, step)
+        return remote(src.at[at], x.at[b, at], right_s.at[b, i], x_r.at[b, i],
+                      {"adapter": lax.rem(a + 1, ZN)})
+
+    def to_left(src, b, i):
+        at = pl.ds(i * step, step)
+        return remote(src.at[at], x.at[b, at], left_s.at[b, i], x_r.at[b, i],
+                      {"adapter": lax.rem(a + ZN - 1, ZN)})
+
+    for i in range(CHUNKS):
+        @pl.when(a < ZN - 1)
+        def _():
+            to_right(tok_ref, a, i).start()
+
+        @pl.when(a > 0)
+        def _():
+            to_left(tok_ref, a, i).start()
 
     part = ball.shape[1] // (2 * ZN)
     p = 2 * t + g
@@ -202,7 +211,7 @@
     r_src = pl.ds(pl.multiple_of((2 * core + g) * part, part), part)
 
     def ids_copy(d):
-        return remote(ids_ref, ids.at[a], ids_s.at[d], ids_r.at[a], {"adapter": zdev[d]})
+        return remote(ids.at[a], ids.at[a], ids_s.at[d], ids_r.at[a], {"adapter": zdev[d]})
 
     def bq_copy(d):
         at = pl.ds(pl.multiple_of(zdev[d] * qcols, 128), qcols)
@@ -241,13 +250,25 @@
         ids_b = jnp.broadcast_to(ids[b][0:1, :], (rows, 128))
         return jnp.sum(jnp.where(lane == row, ids_b, 0), axis=1, keepdims=True)
 
-    def part_copy(b):
-        return remote(send.at[b], recv.at[t], part_s.at[b], part_r.at[t], {"tensor": b})
+    half = cols // 2
+    here = t // 2
+    mine_at = pl.ds(pl.multiple_of(core * half, 128), half)
+    other_at = pl.ds(pl.multiple_of((1 - core) * half, 128), half)
+
+    def pair_copy(b):
+        return remote(pair_send.at[b], pair_recv.at[b], pair_s.at[b], pair_r.at[b], {"tensor": sibling})
+
+    def far_copy(b):
+        return remote(far_send.at[b], far_recv.at[core], far_s.at[b], far_r.at[core], {"tensor": b})
+
+    def near_copy():
+        return remote(near_send, near_recv, near_s.at[0], near_r.at[0], {"tensor": sibling})
 
     def low_copy(b):
         return remote(low_send.at[b], low_recv.at[t], low_s.at[b], low_r.at[t], {"tensor": b})
 
-    tile = 256
+    def times(b, at):
+        return jnp.dot(x[b], wd[:, at], preferred_element_type=jnp.float32)
 
     def compute(b):
         both = jnp.dot(x[b], wd[:, cols:], preferred_element_type=jnp.float32)
@@ -261,49 +282,58 @@
         def _():
             low_copy(b).start()
 
-            @pl.loop(0, cols // tile)
+        @pl.when(b // 2 != here)
+        def _():
+            pair_send[b] = times(b, other_at).astype(jnp.bfloat16)
+            pair_copy(b).start()
+            held[...] = times(b, mine_at)
+            pair_copy(b).wait_recv()
+            far_send[b] = (held[...] + pair_recv[b].astype(jnp.float32)).astype(jnp.bfloat16)
+            far_copy(b).start()
+
+        @pl.when(b == sibling)
+        def _():
+            @pl.loop(0, 2)
             def _(n):
-                at = pl.ds(pl.multiple_of(n * tile, tile), tile)
-                send[b, :, at] = jnp.dot(
-                    x[b], wd[:, at], preferred_element_type=jnp.float32
-                ).astype(jnp.bfloat16)
-
-            part_copy(b).start()
+                at = pl.ds(pl.multiple_of(n * half, 128), half)
+                near_send[:, at] = times(b, at).astype(jnp.bfloat16)
+
+            near_copy().start()
 
         @pl.when(b == t)
         def _():
-            @pl.loop(0, cols // tile)
+            @pl.loop(0, 2)
             def _(n):
-                at = pl.ds(pl.multiple_of(n * tile, tile), tile)
-                base[:, at] = jnp.dot(x[b], wd[:, at], preferred_element_type=jnp.float32)
+                at = pl.ds(pl.multiple_of(n * half, 128), half)
+                base[:, at] = times(b, at)
 
     for copy in loads:
         copy.wait()
     compute(a)
 
-    for d in range(1, ZN):
-        bq_copy(d).wait_recv()
-        bv_copy(d).wait_recv()
-    y_copy().start()
-
     for s in range(1, ZN):
         lo, hi = a - s, a + s
-
-        @pl.when(lo >= 0)
-        def _():
-            to_right(tok_ref, lo).wait_recv()
-
-            @pl.when(a < ZN - 1)
+        for i in range(CHUNKS):
+            @pl.when(lo >= 0)
             def _():
-                to_right(x.at[lo], lo).start()
-
-        @pl.when(hi < ZN)
-        def _():
-            to_left(tok_ref, hi).wait_recv()
-
-            @pl.when(a > 0)
+                to_right(tok_ref, lo, i).wait_recv()
+
+                @pl.when(a < ZN - 1)
+                def _():
+                    to_right(x.at[lo], lo, i).start()
+
+            @pl.when(hi < ZN)
             def _():
-                to_left(x.at[hi], hi).start()
+                to_left(tok_ref, hi, i).wait_recv()
+
+                @pl.when(a > 0)
+                def _():
+                    to_left(x.at[hi], hi, i).start()
+
+        if s == 2:
+            y_in = ball.at[pl.ds(0, ZN - 1), pl.ds(pl.multiple_of((2 * t + 1 - g) * part, part), part), :]
+            remote(y_in, y_in, plane_s.at[0], plane_r.at[0], {"groups": 1 - g}).wait_recv()
+            x_copy(t).start()
 
         @pl.loop(0, 2)
         def _(way):
@@ -311,14 +341,15 @@
 
             @pl.when((b >= 0) & (b < ZN))
             def _():
-                remote(ids_ref, ids.at[b], ids_s.at[1], ids_r.at[b], {"adapter": zdev[1]}).wait_recv()
+                remote(ids.at[b], ids.at[b], ids_s.at[1], ids_r.at[b], {"adapter": zdev[1]}).wait_recv()
                 compute(b)
 
         if s == 1:
-            y_copy_in = ball.at[pl.ds(0, ZN - 1), pl.ds(pl.multiple_of((2 * t + 1 - g) * part, part), part), :]
-            remote(y_copy_in, y_copy_in, plane_s.at[0], plane_r.at[0], {"groups": 1 - g}).wait_recv()
-            x_copy(t).start()
-        if s == 2:
+            for d in range(1, ZN):
+                bq_copy(d).wait_recv()
+                bv_copy(d).wait_recv()
+            y_copy().start()
+        if s == 3:
             x_copy(xpeer).wait_recv()
             core_copy(0, t).start()
             core_copy(1, xpeer).start()
@@ -354,15 +385,16 @@
         lv.append(jnp.where(hit, wide_v, 0.0).astype(jnp.bfloat16))
     lq = jnp.concatenate(lq, axis=1)
     lv = jnp.concatenate(lv, axis=1)
-    for d in range(1, ZN):
-        remote(send.at[0], recv.at[tdev[d]], part_s.at[0], part_r.at[tdev[d]], {"tensor": tdev[d]}).wait_recv()
+    near_copy().wait_recv()
+    for h in range(2):
+        remote(far_recv.at[h], far_recv.at[h], far_s.at[0], far_r.at[h], {"tensor": xpeer}).wait_recv()
 
     def finish(at, low_rows, b_at, width):
         factors = ball[:, :, b_at : b_at + width].reshape(ZN * 2 * rank, width)
         delta = jnp.dot(low_rows, factors, preferred_element_type=jnp.float32)
-        val = base[:, at : at + width]
-        for d in range(1, ZN):
-            val = val + recv[tdev[d], :, at : at + width].astype(jnp.float32)
+        val = base[:, at : at + width] + near_recv[:, at : at + width].astype(jnp.float32)
+        far = far_recv[at // half, :, at % half : at % half + width]
+        val = val + far.astype(jnp.float32)
         delta = delta.astype(jnp.bfloat16).astype(jnp.float32)
         out_ref[:, at : at + width] = (val + delta).astype(jnp.bfloat16)
 
@@ -375,22 +407,29 @@
     def _(b):
         @pl.when((b <= a) & (a < ZN - 1))
         def _():
-            to_right(tok_ref, b).wait_send()
+            for i in range(CHUNKS):
+                to_right(tok_ref, b, i).wait_send()
 
         @pl.when((b >= a) & (a > 0))
         def _():
-            to_left(tok_ref, b).wait_send()
+            for i in range(CHUNKS):
+                to_left(tok_ref, b, i).wait_send()
 
         @pl.when(b != t)
         def _():
-            part_copy(b).wait_send()
             low_copy(b).wait_send()
+
+        @pl.when(b // 2 != here)
+        def _():
+            pair_copy(b).wait_send()
+            far_copy(b).wait_send()
 
     for d in range(1, ZN):
         ids_copy(d).wait_send()
         bq_copy(d).wait_send()
         bv_copy(d).wait_send()
         lz_copy(d).wait_send()
+    near_copy().wait_send()
     y_copy().wait_send()
     x_copy(t).wait_send()
     core_copy(0, t).wait_send()
@@ -401,10 +440,10 @@
     rows, feats = tokens.shape
     cols = weight.shape[1]
     rank2 = down.shape[2]
-    ids = jnp.broadcast_to(jnp.pad(index_rows, (0, 128 - rows))[None, :], (8, 128))
+    ids = index_rows[None, :]
     dma = pltpu.SemaphoreType.DMA
     vmem = pltpu.VMEM
-    any_spec = pl.BlockSpec(memory_space=pl.ANY)
+    any_spec = pl.BlockSpec(memory_space=pltpu.HBM)
     return pl.pallas_call(
         fused_kernel,
         out_shape=jax.ShapeDtypeStruct((rows, cols), jnp.bfloat16),
@@ -413,17 +452,22 @@
         scratch_shapes=[
             vmem((ZN, rows, feats), jnp.bfloat16),
             vmem((feats, cols + 2 * rank2), jnp.bfloat16),
-            vmem((ZN, rows, cols), jnp.bfloat16),
-            vmem((ZN, rows, cols), jnp.bfloat16),
+            vmem((ZN, rows, cols // 2), jnp.bfloat16),
+            vmem((ZN, rows, cols // 2), jnp.bfloat16),
+            vmem((ZN, rows, cols // 2), jnp.bfloat16),
+            vmem((2, rows, cols // 2), jnp.bfloat16),
+            vmem((rows, cols), jnp.bfloat16),
+            vmem((rows, cols), jnp.bfloat16),
+            vmem((rows, cols // 2), jnp.float32),
             vmem((rows, cols), jnp.float32),
             vmem((ZN, rows, rank2), jnp.float32),
             vmem((ZN, rows, rank2), jnp.float32),
             vmem((ZN, rows, rank2), jnp.bfloat16),
             vmem((ZN, rank2, cols), jnp.bfloat16),
             vmem((ZN, 8, 128), jnp.int32),
-        ] + [dma((4,))] * 19,
+        ] + [dma((ZN,))] * 20 + [dma((ZN, CHUNKS))] * 3,
         compiler_params=pltpu.CompilerParams(
-            collective_id=0, has_side_effects=True, vmem_limit_bytes=48 * 1024 * 1024
+            collective_id=0, has_side_effects=True, vmem_limit_bytes=62 * 1024 * 1024
         ),
     )(tokens, weight, down, bq, bv, ids)
 

time: 64.1 us -> 56.5 us (0.88)
  the two profiles are of different devices: /device:TPU:11 before, /device:TPU:0 now
where the time goes in v2:
time: 56.5 us; the launch traced here: 56.4 us
  Pallas kernels  54.6 us (97%)
  local copies, waits for them, and re-layouts  1.8 us (3%)
    pallas_call x1, Pallas kernels, fused_on_device(): pl.pallas_call(fused_kernel, out_shape=jax.ShapeDtypeStruct((rows, cols),...  54.6 us
    unnamed x1, local copies, waits for them, and re-layouts  1.8 us

profile of v2, /device:TPU:0, one launch (start us, length us, event | category | flops | bytes accessed | tf_op | source)
XLA Modules:
  0.0 56.4 jit_solution(18244074635535290921)
XLA Ops:
  0.0 54.6 %shard_map.64 = bf16[96,2304]{1,0:T(8,128)(2,1)} custom-call(bf16[96,2048]{1,0:T(8,128)(2,1)} %tok_ref.1, bf16[2048,2304]{1,0:T(8,128)(2,1)} %w_ref.1, bf16[2,2048,128]{2,1,0:T(8,128)(2,1)} %down_ref.1, bf16[2,64,8192]{2,1,0:T(8,128)(2,1)} %bq_ref.1, bf16[2,64,1024]{2,1,0:T(8,128)(2,1)} %bv_ref.1, s32[1,96]{1,0:T(1,128)} %bitcast.1), custom_call_target="tpu_custom_call" | custom-call | tf_op jit(solution)/shard_map/pallas_call | solution.py:447
  54.6 1.8 %copy.8 = bf16[96,2304]{1,0:T(8,128)(2,1)} copy(bf16[96,2304]{1,0:T(8,128)(2,1)} %shard_map.64) | data formatting | bytes 884736

commit v3 on v2

--- a/solution.py
+++ b/solution.py
@@ -133,8 +133,8 @@
 def fused_kernel(
     tok_ref, w_ref, down_ref, bq_ref, bv_ref, ids_ref, out_ref,
     x, wd, pair_send, pair_recv, far_send, far_recv, near_send, near_recv, held, base, low_send, low_recv, low_z, ball, ids,
-    load_sem, own_sem, ids_s, ids_r, pair_s, pair_r, far_s, far_r, near_s, near_r,
-    low_s, low_r, lz_s, lz_r, bqz_s, bqz_r, bvz_s, bvz_r, plane_s, plane_r, right_s, left_s, x_r,
+    load_sem, own_sem, ids_s, ids_r, pair_s, far_s, far_r, near_s, near_r,
+    low_s, low_r, lz_s, lz_r, bqz_s, bqz_r, bvz_s, bvz_r, plane_s, plane_r, right_s, left_s, x_r, pair_r,
 ):
     g = lax.axis_index("groups")
     a = lax.axis_index("adapter")
@@ -183,27 +183,6 @@
     pl.semaphore_signal(barrier, inc=1, device_id={"groups": 1 - g}, device_id_type=MESH)
     pl.semaphore_wait(barrier, 2 * ZN - 1)
 
-    step = rows // CHUNKS
-
-    def to_right(src, b, i):
-        at = pl.ds(i * step, step)
-        return remote(src.at[at], x.at[b, at], right_s.at[b, i], x_r.at[b, i],
-                      {"adapter": lax.rem(a + 1, ZN)})
-
-    def to_left(src, b, i):
-        at = pl.ds(i * step, step)
-        return remote(src.at[at], x.at[b, at], left_s.at[b, i], x_r.at[b, i],
-                      {"adapter": lax.rem(a + ZN - 1, ZN)})
-
-    for i in range(CHUNKS):
-        @pl.when(a < ZN - 1)
-        def _():
-            to_right(tok_ref, a, i).start()
-
-        @pl.when(a > 0)
-        def _():
-            to_left(tok_ref, a, i).start()
-
     part = ball.shape[1] // (2 * ZN)
     p = 2 * t + g
     p_rows = pl.ds(pl.multiple_of(p * part, part), part)
@@ -229,6 +208,27 @@
         bq_copy(d).start()
         bv_copy(d).start()
 
+    step = rows // CHUNKS
+
+    def to_right(src, b, i):
+        at = pl.ds(i * step, step)
+        return remote(src.at[at], x.at[b, at], right_s.at[b, i], x_r.at[b, i],
+                      {"adapter": lax.rem(a + 1, ZN)})
+
+    def to_left(src, b, i):
+        at = pl.ds(i * step, step)
+        return remote(src.at[at], x.at[b, at], left_s.at[b, i], x_r.at[b, i],
+                      {"adapter": lax.rem(a + ZN - 1, ZN)})
+
+    for i in range(CHUNKS):
+        @pl.when(a < ZN - 1)
+        def _():
+            to_right(tok_ref, a, i).start()
+
+        @pl.when(a > 0)
+        def _():
+            to_left(tok_ref, a, i).start()
+
     def y_copy():
         ref = ball.at[pl.ds(0, ZN - 1), p_rows, :]
         return remote(ref, ref, plane_s.at[0], plane_r.at[0], {"groups": 1 - g})
@@ -255,11 +255,13 @@
     mine_at = pl.ds(pl.multiple_of(core * half, 128), half)
     other_at = pl.ds(pl.multiple_of((1 - core) * half, 128), half)
 
-    def pair_copy(b):
-        return remote(pair_send.at[b], pair_recv.at[b], pair_s.at[b], pair_r.at[b], {"tensor": sibling})
-
-    def far_copy(b):
-        return remote(far_send.at[b], far_recv.at[core], far_s.at[b], far_r.at[core], {"tensor": b})
+    def pair_copy(b, at, piece):
+        return remote(pair_send.at[b, at], pair_recv.at[b, at], pair_s.at[b], pair_r.at[b, piece],
+                      {"tensor": sibling})
+
+    def far_copy(b, at):
+        return remote(far_send.at[b, at], far_recv.at[core, at], far_s.at[b], far_r.at[core],
+                      {"tensor": b})
 
     def near_copy():
         return remote(near_send, near_recv, near_s.at[0], near_r.at[0], {"tensor": sibling})
@@ -267,51 +269,65 @@
     def low_copy(b):
         return remote(low_send.at[b], low_recv.at[t], low_s.at[b], low_r.at[t], {"tensor": b})
 
-    def times(b, at):
-        return jnp.dot(x[b], wd[:, at], preferred_element_type=jnp.float32)
-
-    def compute(b):
-        both = jnp.dot(x[b], wd[:, cols:], preferred_element_type=jnp.float32)
-        id_col = column(b)
-        zero = jnp.zeros((rows, 2 * rank), jnp.float32)
+    whole = pl.ds(0, rows)
+
+    def compute(b, r0, n, piece):
+        at_rows = pl.ds(r0, n)
+        last = r0 + n == rows
+
+        def times(at):
+            return jnp.dot(x[b, at_rows], wd[:, at], preferred_element_type=jnp.float32)
+
+        both = times(pl.ds(cols, 4 * rank))
+        id_col = column(b)[r0 : r0 + n]
+        zero = jnp.zeros((n, 2 * rank), jnp.float32)
         low = jnp.where(id_col == 2 * a, both[:, : 2 * rank], zero)
         low = jnp.where(id_col == 2 * a + 1, both[:, 2 * rank :], low)
-        low_send[b] = low
-
-        @pl.when(b != t)
-        def _():
-            low_copy(b).start()
+        low_send[b, at_rows] = low
+
+        if last:
+            @pl.when(b != t)
+            def _():
+                low_copy(b).start()
 
         @pl.when(b // 2 != here)
         def _():
-            pair_send[b] = times(b, other_at).astype(jnp.bfloat16)
-            pair_copy(b).start()
-            held[...] = times(b, mine_at)
-            pair_copy(b).wait_recv()
-            far_send[b] = (held[...] + pair_recv[b].astype(jnp.float32)).astype(jnp.bfloat16)
-            far_copy(b).start()
+            pair_send[b, at_rows] = times(other_at).astype(jnp.bfloat16)
+            pair_copy(b, at_rows, piece).start()
+            held[at_rows] = times(mine_at)
+            pair_copy(b, at_rows, piece).wait_recv()
+            far_send[b, at_rows] = (
+                held[at_rows] + pair_recv[b, at_rows].astype(jnp.float32)
+            ).astype(jnp.bfloat16)
+            far_copy(b, at_rows).start()
 
         @pl.when(b == sibling)
         def _():
             @pl.loop(0, 2)
-            def _(n):
-                at = pl.ds(pl.multiple_of(n * half, 128), half)
-                near_send[:, at] = times(b, at).astype(jnp.bfloat16)
-
-            near_copy().start()
+            def _(m):
+                at = pl.ds(pl.multiple_of(m * half, 128), half)
+                near_send[at_rows, at] = times(at).astype(jnp.bfloat16)
+
+            if last:
+                near_copy().start()
 
         @pl.when(b == t)
         def _():
             @pl.loop(0, 2)
-            def _(n):
-                at = pl.ds(pl.multiple_of(n * half, 128), half)
-                base[:, at] = times(b, at)
+            def _(m):
+                at = pl.ds(pl.multiple_of(m * half, 128), half)
+                base[at_rows, at] = times(at)
 
     for copy in loads:
         copy.wait()
-    compute(a)
-
-    for s in range(1, ZN):
+    compute(a, 0, rows, 0)
+
+    for d in range(1, ZN):
+        bq_copy(d).wait_recv()
+        bv_copy(d).wait_recv()
+    y_copy().start()
+
+    for s in range(1, ZN - 1):
         lo, hi = a - s, a + s
         for i in range(CHUNKS):
             @pl.when(lo >= 0)
@@ -330,10 +346,11 @@
                 def _():
                     to_left(x.at[hi], hi, i).start()
 
-        if s == 2:
+        if s == 1:
             y_in = ball.at[pl.ds(0, ZN - 1), pl.ds(pl.multiple_of((2 * t + 1 - g) * part, part), part), :]
             remote(y_in, y_in, plane_s.at[0], plane_r.at[0], {"groups": 1 - g}).wait_recv()
             x_copy(t).start()
+            core_copy(0, t).start()
 
         @pl.loop(0, 2)
         def _(way):
@@ -342,17 +359,21 @@
             @pl.when((b >= 0) & (b < ZN))
             def _():
                 remote(ids.at[b], ids.at[b], ids_s.at[1], ids_r.at[b], {"adapter": zdev[1]}).wait_recv()
-                compute(b)
-
-        if s == 1:
-            for d in range(1, ZN):
-                bq_copy(d).wait_recv()
-                bv_copy(d).wait_recv()
-            y_copy().start()
-        if s == 3:
-            x_copy(xpeer).wait_recv()
-            core_copy(0, t).start()
-            core_copy(1, xpeer).start()
+                compute(b, 0, rows, 0)
+
+
+    x_copy(xpeer).wait_recv()
+    core_copy(1, xpeer).start()
+
+    far_end = ZN - 1 - a
+
+    @pl.when((a == 0) | (a == ZN - 1))
+    def _():
+        remote(ids.at[far_end], ids.at[far_end], ids_s.at[1], ids_r.at[far_end],
+               {"adapter": zdev[1]}).wait_recv()
+        for i in range(CHUNKS):
+            to_left(tok_ref, far_end, i).wait_recv()
+        compute(far_end, 0, rows, 0)
 
     total = low_send[t]
     for d in range(1, ZN):
@@ -386,22 +407,23 @@
     lq = jnp.concatenate(lq, axis=1)
     lv = jnp.concatenate(lv, axis=1)
     near_copy().wait_recv()
+
+    def add_delta(at, low_rows, b_at, width):
+        factors = ball[:, :, b_at : b_at + width].reshape(ZN * 2 * rank, width)
+        delta = jnp.dot(low_rows, factors, preferred_element_type=jnp.float32)
+        delta = delta.astype(jnp.bfloat16).astype(jnp.float32)
+        near = near_recv[:, at : at + width].astype(jnp.float32)
+        base[:, at : at + width] = base[:, at : at + width] + near + delta
+
+    for grp in range(groups_here):
+        for c in range(qg // 256):
+            add_delta(grp * (qg + vg) + c * 256, lq, grp * qg + c * 256, 256)
+        add_delta(grp * (qg + vg) + qg, lv, qcols + grp * vg, vg)
+
     for h in range(2):
         remote(far_recv.at[h], far_recv.at[h], far_s.at[0], far_r.at[h], {"tensor": xpeer}).wait_recv()
-
-    def finish(at, low_rows, b_at, width):
-        factors = ball[:, :, b_at : b_at + width].reshape(ZN * 2 * rank, width)
-        delta = jnp.dot(low_rows, factors, preferred_element_type=jnp.float32)
-        val = base[:, at : at + width] + near_recv[:, at : at + width].astype(jnp.float32)
-        far = far_recv[at // half, :, at % half : at % half + width]
-        val = val + far.astype(jnp.float32)
-        delta = delta.astype(jnp.bfloat16).astype(jnp.float32)
-        out_ref[:, at : at + width] = (val + delta).astype(jnp.bfloat16)
-
-    for grp in range(groups_here):
-        for c in range(qg // 256):
-            finish(grp * (qg + vg) + c * 256, lq, grp * qg + c * 256, 256)
-        finish(grp * (qg + vg) + qg, lv, qcols + grp * vg, vg)
+        at = pl.ds(h * half, half)
+        out_ref[:, at] = (base[:, at] + far_recv[h].astype(jnp.float32)).astype(jnp.bfloat16)
 
     @pl.loop(0, ZN)
     def _(b):
@@ -421,8 +443,8 @@
 
         @pl.when(b // 2 != here)
         def _():
-            pair_copy(b).wait_send()
-            far_copy(b).wait_send()
+            pair_copy(b, whole, 0).wait_send()
+            far_copy(b, whole).wait_send()
 
     for d in range(1, ZN):
         ids_copy(d).wait_send()
@@ -465,7 +487,7 @@
             vmem((ZN, rows, rank2), jnp.bfloat16),
             vmem((ZN, rank2, cols), jnp.bfloat16),
             vmem((ZN, 8, 128), jnp.int32),
-        ] + [dma((ZN,))] * 20 + [dma((ZN, CHUNKS))] * 3,
+        ] + [dma((ZN,))] * 19 + [dma((ZN, CHUNKS))] * 4,
         compiler_params=pltpu.CompilerParams(
             collective_id=0, has_side_effects=True, vmem_limit_bytes=62 * 1024 * 1024
         ),

time: 56.5 us -> 50.6 us (0.90)
  Pallas kernels: 54.6 us -> 48.6 us
    pallas_call x1, Pallas kernels: 54.6 us -> 48.6 us  [fused_on_device(): pl.pallas_call(fused_kernel, out_shape=jax.ShapeDtypeStruct((rows, cols),...]
where the time goes in v3:
time: 50.6 us; the launch traced here: 50.4 us
  Pallas kernels  48.6 us (96%)
  local copies, waits for them, and re-layouts  1.8 us (4%)
    pallas_call x1, Pallas kernels, fused_on_device(): pl.pallas_call(fused_kernel, out_shape=jax.ShapeDtypeStruct((rows, cols),...  48.6 us
    unnamed x1, local copies, waits for them, and re-layouts  1.8 us

profile of v3, /device:TPU:0, one launch (start us, length us, event | category | flops | bytes accessed | tf_op | source)
XLA Modules:
  0.0 50.4 jit_solution(7923307950533064433)
XLA Ops:
  0.0 48.6 %shard_map.64 = bf16[96,2304]{1,0:T(8,128)(2,1)} custom-call(bf16[96,2048]{1,0:T(8,128)(2,1)} %tok_ref.1, bf16[2048,2304]{1,0:T(8,128)(2,1)} %w_ref.1, bf16[2,2048,128]{2,1,0:T(8,128)(2,1)} %down_ref.1, bf16[2,64,8192]{2,1,0:T(8,128)(2,1)} %bq_ref.1, bf16[2,64,1024]{2,1,0:T(8,128)(2,1)} %bv_ref.1, s32[1,96]{1,0:T(1,128)} %bitcast.1), custom_call_target="tpu_custom_call" | custom-call | tf_op jit(solution)/shard_map/pallas_call | solution.py:469
  48.6 1.8 %copy.8 = bf16[96,2304]{1,0:T(8,128)(2,1)} copy(bf16[96,2304]{1,0:T(8,128)(2,1)} %shard_map.64) | data formatting | bytes 884736
